TPU v7x, 128 devices: a whole 4x4x4 slice. The times are simulated.
128 devices in a mesh: ctx: 8 (over z_hi, x), exp: 16 (over y, z_lo, core).
Axes of the slice: x: 4, y: 4, z: 4 (z_hi: 2, z_lo: 2; z = z_hi * 2 + z_lo), core: 2. Of those that a mesh axis runs over, the one named last changes fastest.
Arguments:
- hidden_in: bfloat16 [16, 1024, 768], P('exp', 'ctx'), may hold values from -6 to 6
- out_grad: bfloat16 [16, 1024, 768], P('exp', 'ctx'), may hold values from -6 to 6
- attn_norm: float32 [768], replicated, may hold values from 0.1 to 1.9
- attn_weight: bfloat16 [3072, 768], P(('ctx', 'exp')), may hold values from -0.8660254 to 0.8660254
- bias_table: float32 [32, 12], replicated, may hold values from -4 to 4
- moe_norm: float32 [768], replicated, may hold values from 0.1 to 1.9
- router: float32 [768, 16], replicated, may hold values from -0.109375 to 0.109375
- expert_in: bfloat16 [16, 768, 3072], P('exp'), may hold values from -0.21875 to 0.21875
- expert_out: bfloat16 [16, 3072, 768], P('exp'), may hold values from -3.5 to 3.5
- expert_ids: int32 [16, 1024, 1], P('exp', 'ctx'), may hold values from 0 to 15; in each aligned block of 128 rows (0 to 127, 128 to 255, ..., all dimensions but the last counted through in order) at most 16 rows name the same one
- block_order: int32 [16, 16], P('exp'), may hold values from 0 to 15, each once within a row
Outputs:
- block_out: bfloat16 [16, 1024, 768], P('exp', 'ctx')
- input_grad: float32 [16, 1024, 768], P('exp', 'ctx')
- attn_norm_grad: float32 [768], replicated
- attn_weight_grad: float32 [3072, 768], P(('ctx', 'exp'))
- bias_table_grad: float32 [32, 12], replicated
- moe_norm_grad: float32 [768], replicated
- router_grad: float32 [768, 16], replicated
- expert_in_grad: float32 [16, 768, 3072], P('exp', 'ctx')
- expert_out_grad: float32 [16, 3072, 768], P('exp', 'ctx')
Inputs may be any that keep to these rules, and one draw needn't show every extreme that they name: `expert_ids`: among the 128 stored rows of one sequence on one index of ctx, at most 16 name the same expert, and in every draw some expert is named by exactly 16 rows of some such block. `block_order`: each sequence's row names every stored block's place once.
All inputs are finite; a program needn't handle non-finite values.
Results may differ from a plain program's by a relative error of at most 0.02.
Values may be sent and summed in bfloat16 or wider, within the bound.
No kernel may reach another device: no remote copies, remote signals or barrier semaphores. Data moves between devices by JAX's collectives and lax.ppermute only.
A program may use at most 128 MiB of HBM per device.

v0:
```python
from functools import partial
import math

import jax
import jax.numpy as jnp
from jax import lax
from jax.sharding import PartitionSpec as P

eps_norm = 1e-06
highest = lax.Precision.HIGHEST
bucket_edges = [
    edge if edge <= 16 else int(math.ceil(16.0 * 8.0 ** ((edge - 16) / 16.0)))
    for edge in range(1, 32)
]


def rms_scaled(values, gain):
    return values * lax.rsqrt(jnp.mean(values * values, axis=-1, keepdims=True) + eps_norm) * gain


def bucketed(distance):
    clipped = jnp.maximum(distance, 0)
    counted = jnp.zeros(distance.shape, jnp.int32)
    for edge in bucket_edges:
        counted = counted + (clipped >= edge).astype(jnp.int32)
    return counted


def head_scores(query_part, key_part, bias_terms, causal):
    raw_scores = (
        jnp.einsum("qhe,khe->hqk", query_part, key_part, preferred_element_type=jnp.float32) * 0.125
    )
    return jnp.where(causal[None], raw_scores + bias_terms, -1e30)


def body(
    hidden_in,
    out_grad,
    attn_norm,
    attn_weight,
    bias_table,
    moe_norm,
    router,
    expert_in,
    expert_out,
    expert_ids,
    block_order,
):
    width_model = attn_norm.shape[0]
    head_count = bias_table.shape[1]
    bucket_count = bias_table.shape[0]
    head_size = width_model // head_count
    group_width = 4 * head_size
    group_count = head_count // 4
    ctx_count = lax.axis_size("ctx")
    ctx_index = lax.axis_index("ctx")
    exp_count = lax.axis_size("exp")
    local_experts = expert_in.shape[0]
    expert_count = router.shape[1]
    local_tokens = hidden_in.shape[1]
    capacity = 2 * local_tokens // expert_count
    sequence_len = local_tokens * ctx_count
    half_block = local_tokens // 2
    inputs = hidden_in[0].astype(jnp.float32)
    weights = lax.all_gather(attn_weight, ("ctx", "exp"), axis=0, tiled=True).reshape(
        4, width_model, width_model
    )
    normed_one, norm_one_pull = jax.vjp(rms_scaled, inputs, attn_norm)
    normed_low = normed_one.astype(jnp.bfloat16)
    projected = jnp.einsum(
        "td,jdf->jtf", normed_low, weights[:3], preferred_element_type=jnp.float32
    ).astype(jnp.bfloat16)
    queries = projected[0]
    gathered = lax.all_gather(projected[1:], "ctx", axis=1, tiled=True)
    all_keys = gathered[0]
    all_values = gathered[1]
    row_ids = jnp.arange(sequence_len, dtype=jnp.int32)
    positions = block_order[0][row_ids // half_block] * half_block + row_ids % half_block
    query_pos = lax.dynamic_slice_in_dim(positions, ctx_index * local_tokens, local_tokens, 0)
    distance = query_pos[:, None] - positions[None, :]
    causal = distance >= 0
    bucket_ids = bucketed(distance)
    one_hot_wide = (bucket_ids[:, :, None] == jnp.arange(bucket_count, dtype=jnp.int32)).astype(
        jnp.float32
    )
    bias_all = jnp.einsum("qkb,bh->hqk", one_hot_wide, bias_table, precision=highest)
    one_hot = one_hot_wide.astype(jnp.bfloat16)

    def group_parts(group_index, sources):
        columns = slice(group_index * group_width, (group_index + 1) * group_width)
        return [source[:, columns].reshape(source.shape[0], 4, head_size) for source in sources]

    def group_bias(group_index):
        return bias_all[group_index * 4 : (group_index + 1) * 4]

    outputs_list = []
    log_totals = []
    for group_index in range(group_count):
        query_part, key_part, value_part = group_parts(group_index, (queries, all_keys, all_values))
        scores = head_scores(query_part, key_part, group_bias(group_index), causal)
        row_peak = jnp.max(scores, axis=-1, keepdims=True)
        log_total = row_peak + jnp.log(jnp.sum(jnp.exp(scores - row_peak), axis=-1, keepdims=True))
        weights_low = jnp.exp(scores - log_total).astype(jnp.bfloat16)
        group_out = jnp.einsum(
            "hqk,khe->qhe", weights_low, value_part, preferred_element_type=jnp.float32
        )
        outputs_list.append(group_out.reshape(local_tokens, group_width))
        log_totals.append(log_total)
    attended = jnp.concatenate(outputs_list, axis=1).astype(jnp.bfloat16)
    attn_out = jnp.dot(attended, weights[3], preferred_element_type=jnp.float32)
    mid_stream = inputs + attn_out
    normed_two, norm_two_pull = jax.vjp(rms_scaled, mid_stream, moe_norm)
    logits = jnp.dot(normed_two, router, precision=highest)
    router_prob = jax.nn.softmax(logits, axis=-1)
    chosen = expert_ids[0, :, 0]
    picked = chosen[:, None] == jnp.arange(expert_count, dtype=jnp.int32)[None, :]
    gate_value = jnp.sum(jnp.where(picked, router_prob, 0.0), axis=-1)
    ranks = jnp.cumsum(picked.astype(jnp.int32), axis=0) - 1
    slot_ids = jnp.sum(jnp.where(picked, ranks, 0), axis=-1)
    targets = chosen * capacity + slot_ids
    placing = (
        targets[:, None] == jnp.arange(expert_count * capacity, dtype=jnp.int32)[None, :]
    ).astype(jnp.bfloat16)
    buffer_shape = (exp_count, local_experts, capacity, width_model)

    def to_slots(rows_low):
        placed = lax.dot_general(
            placing, rows_low, (((0,), (0,)), ((), ())), preferred_element_type=jnp.float32
        )
        return placed.astype(jnp.bfloat16).reshape(buffer_shape)

    def from_slots(slot_rows):
        return jnp.dot(
            placing,
            slot_rows.reshape(expert_count * capacity, width_model),
            preferred_element_type=jnp.float32,
        )

    outgoing = to_slots(normed_two.astype(jnp.bfloat16))
    arrived_rows = lax.all_to_all(outgoing, "exp", split_axis=0, concat_axis=0, tiled=True)
    pre_act = jnp.einsum(
        "sekd,edf->sekf", arrived_rows, expert_in, preferred_element_type=jnp.float32
    )
    activated = jax.nn.gelu(pre_act, approximate=True).astype(jnp.bfloat16)
    produced = jnp.einsum(
        "sekf,efd->sekd", activated, expert_out, preferred_element_type=jnp.float32
    ).astype(jnp.bfloat16)
    produced, pre_act, activated, arrived_rows = (produced, pre_act, activated, arrived_rows)
    returned_rows = lax.all_to_all(produced, "exp", split_axis=0, concat_axis=0, tiled=True)
    expert_result = from_slots(returned_rows)
    block_out = (mid_stream + gate_value[:, None] * expert_result).astype(jnp.bfloat16)[None]
    cotangent = out_grad[0].astype(jnp.float32)
    scaled_grad = (gate_value[:, None] * cotangent).astype(jnp.bfloat16)
    gate_grad = jnp.sum(cotangent * expert_result, axis=-1)
    prob_grad = jnp.where(picked, gate_grad[:, None], 0.0)
    logit_grad = router_prob * (
        prob_grad - jnp.sum(router_prob * prob_grad, axis=-1, keepdims=True)
    )
    router_local = jnp.dot(normed_two.T, logit_grad, precision=highest)
    routed_back = jnp.dot(logit_grad, router.T, precision=highest)
    grad_outgoing = to_slots(scaled_grad)
    result_grad = lax.all_to_all(grad_outgoing, "exp", split_axis=0, concat_axis=0, tiled=True)
    hidden_grad = jnp.einsum(
        "sekd,efd->sekf", result_grad, expert_out, preferred_element_type=jnp.float32
    )
    gelu_pull = jax.vjp(partial(jax.nn.gelu, approximate=True), pre_act)[1]
    pre_grad = gelu_pull(hidden_grad)[0].astype(jnp.bfloat16)
    row_grad = jnp.einsum(
        "sekf,edf->sekd", pre_grad, expert_in, preferred_element_type=jnp.float32
    ).astype(jnp.bfloat16)
    returned_grad = lax.all_to_all(row_grad, "exp", split_axis=0, concat_axis=0, tiled=True)
    input_rows_grad = from_slots(returned_grad)
    in_local = jnp.einsum(
        "sekd,sekf->edf", arrived_rows, pre_grad, preferred_element_type=jnp.float32
    )
    out_local = jnp.einsum(
        "sekf,sekd->efd", activated, result_grad, preferred_element_type=jnp.float32
    )
    expert_in_grad, expert_out_grad = (
        lax.psum_scatter(
            in_local.astype(jnp.bfloat16), "ctx", scatter_dimension=1, tiled=True
        ).astype(jnp.float32),
        lax.psum_scatter(
            out_local.astype(jnp.bfloat16), "ctx", scatter_dimension=1, tiled=True
        ).astype(jnp.float32),
    )
    mid_part, moe_norm_local = norm_two_pull(input_rows_grad + routed_back)
    mid_grad = cotangent + mid_part
    attn_grad = mid_grad.astype(jnp.bfloat16)
    out_weight_grad = lax.dot_general(
        attended, attn_grad, (((0,), (0,)), ((), ())), preferred_element_type=jnp.float32
    )
    attended_grad = lax.dot_general(
        attn_grad, weights[3], (((1,), (1,)), ((), ())), preferred_element_type=jnp.float32
    ).astype(jnp.bfloat16)
    query_parts, key_parts, value_parts, table_parts = ([], [], [], [])
    for group_index in range(group_count):
        query_part, key_part, value_part, output_part = group_parts(
            group_index, (queries, all_keys, all_values, attended_grad)
        )
        scores = head_scores(query_part, key_part, group_bias(group_index), causal)
        probs = jnp.exp(scores - log_totals[group_index])
        probs_grad = jnp.einsum(
            "qhe,khe->hqk", output_part, value_part, preferred_element_type=jnp.float32
        )
        row_dot = jnp.sum(probs * probs_grad, axis=-1, keepdims=True)
        score_grad = (probs * (probs_grad - row_dot)).astype(jnp.bfloat16)
        value_parts.append(
            jnp.einsum(
                "hqk,qhe->khe",
                probs.astype(jnp.bfloat16),
                output_part,
                preferred_element_type=jnp.float32,
            ).reshape(sequence_len, group_width)
        )
        query_parts.append(
            (
                jnp.einsum("hqk,khe->qhe", score_grad, key_part, preferred_element_type=jnp.float32)
                * 0.125
            ).reshape(local_tokens, group_width)
        )
        key_parts.append(
            (
                jnp.einsum(
                    "hqk,qhe->khe", score_grad, query_part, preferred_element_type=jnp.float32
                )
                * 0.125
            ).reshape(sequence_len, group_width)
        )
        table_parts.append(
            jnp.einsum("hqk,qkb->bh", score_grad, one_hot, preferred_element_type=jnp.float32)
        )
    kv_terms = jnp.stack([jnp.concatenate(key_parts, axis=1), jnp.concatenate(value_parts, axis=1)])
    kv_local = lax.psum_scatter(
        kv_terms.astype(jnp.bfloat16), "ctx", scatter_dimension=1, tiled=True
    )
    projected_grad = jnp.concatenate(
        [jnp.concatenate(query_parts, axis=1).astype(jnp.bfloat16)[None], kv_local], axis=0
    )
    qkv_weight_grad = jnp.einsum(
        "td,jtf->jdf", normed_low, projected_grad, preferred_element_type=jnp.float32
    )
    normed_grad = jnp.einsum(
        "jtf,jdf->td", projected_grad, weights[:3], preferred_element_type=jnp.float32
    )
    input_part, attn_norm_local = norm_one_pull(normed_grad)
    input_grad = (mid_grad + input_part)[None]
    weight_grad = jnp.concatenate(
        [qkv_weight_grad.reshape(3 * width_model, width_model), out_weight_grad], axis=0
    )
    attn_weight_grad = lax.psum_scatter(
        weight_grad, ("ctx", "exp"), scatter_dimension=0, tiled=True
    )
    summed_small = lax.psum(
        (attn_norm_local, moe_norm_local, router_local, jnp.concatenate(table_parts, axis=1)),
        ("ctx", "exp"),
    )
    return (
        block_out,
        input_grad,
        summed_small[0],
        attn_weight_grad,
        summed_small[3],
        summed_small[1],
        summed_small[2],
        expert_in_grad,
        expert_out_grad,
    )


def solution(mesh):
    placed = (
        P("exp", "ctx", None),
        P("exp", "ctx", None),
        P(),
        P(("ctx", "exp"), None),
        P(),
        P(),
        P(),
        P("exp", None, None),
        P("exp", None, None),
        P("exp", "ctx", None),
        P("exp", None),
    )
    return jax.shard_map(
        body,
        mesh=mesh,
        in_specs=placed,
        out_specs=(
            P("exp", "ctx", None),
            P("exp", "ctx", None),
            P(),
            P(("ctx", "exp"), None),
            P(),
            P(),
            P(),
            P("exp", "ctx", None),
            P("exp", "ctx", None),
        ),
        check_vma=False,
    )
```

profile of v0, /device:TPU:0, one launch (start us, length us, event | category | flops | bytes accessed | tf_op | source)
XLA Modules:
  0.0 1337.1 jit_solution(14222821979344142034)
XLA Ops:
  9.6 202.5 %all-gather.3.cloned.1.call-done = bf16[3072,768]{1,0:T(8,128)(2,1)} async-done(((bf16[24,768]{1,0:T(8,128)(2,1)}), bf16[3072,768]{1,0:T(8,128)(2,1)}) %all-gather.3.cloned.1.call-update) | async-done | bytes 4718608 | tf_op jit(solution)/shard_map/all_gather | solution.py:65
  218.3 4.5 compare_select_fusion.1
  222.8 5.7 fusion.169
  230.5 7.2 fusion
  237.7 8.4 copy.105
  248.5 29.9 %all-gather.5.cloned.1.call-done = bf16[2,1024,768]{2,1,0:T(8,128)(2,1)} async-done(((bf16[2,128,768]{2,1,0:T(8,128)(2,1)}), bf16[2,1024,768]{2,1,0:T(8,128)(2,1)}) %all-gather.5.cloned.1.call-update) | async-done | bytes 3145744 | tf_op jit(solution)/shard_map/all_gather | solution.py:74
  300.5 13.8 %all_to_all.20 = bf16[16,1,16,768]{3,2,1,0:T(8,128)(2,1)S(1)} all-to-all(bf16[16,1,16,768]{3,2,1,0:T(8,128)(2,1)S(1)} %bitcast.317), channel_id=1, replica_groups=mesh['ctx'=8,'exp'=16] {'exp'}, dimensions={0} | all-to-all | bytes 786432 | tf_op jit(solution)/shard_map/all_to_all | solution.py:140
  320.9 4.2 all-to-all-start.1
  325.7 8.6 all-to-all-done.1
  337.3 12.2 all_to_all.21
  349.5 6.8 fusion.33
  357.9 12.0 all_to_all.22
  374.5 3.1 convolution_convert_fusion.3
  380.6 3.1 convolution_convert_fusion.1
  416.7 6.2 fusion.17
  424.5 3.6 fusion.16
  436.8 3.0 fusion.154
  439.8 53.2 %reduce-scatter.5.cloned.1.call-done = bf16[2,128,768]{2,1,0:T(8,128)(2,1)} async-done(((bf16[2,1024,768]{2,1,0:T(8,128)(2,1)}), bf16[2,128,768]{2,1,0:T(8,128)(2,1)}) %reduce-scatter.5.cloned.1.call-update) | async-done | bytes 393232 | tf_op jit(solution)/shard_map/reduce_scatter | solution.py:234
  493.0 5.0 fusion.138
  498.0 8.0 pad_maximum_fusion
  511.8 3.6 fusion.67
  521.4 69.1 %all-reduce = (f32[768]{0:T(1024)}, f32[32,12]{0,1:T(8,128)}, f32[768]{0:T(1024)}, f32[768,16]{0,1:T(8,128)}) all-reduce(f32[768]{0:T(1024)S(1)} %get-tuple-element.11, f32[32,12]{0,1:T(8,128)S(1)} %pad_maximum_fusion.8, f32[768]{0:T(1024)S(1)} %get-tuple-element.9, ...), channel_id=1, replica_groups=mesh['ctx'=8,'exp'=16] {'ctx','exp'}, use_global_device_ids=true, to_apply=%region_22.23 | all-reduce | flops 14208 | bytes 113664 | tf_op jit(solution)/shard_map/psum | solution.py:254
  593.6 82.1 %reduce-scatter.9.cloned.1.call-done = bf16[1,96,3072]{2,1,0:T(8,128)(2,1)} async-done(((bf16[1,768,3072]{2,1,0:T(8,128)(2,1)}), bf16[1,96,3072]{2,1,0:T(8,128)(2,1)}) %reduce-scatter.9.cloned.1.call-update) | async-done | bytes 589840 | tf_op jit(solution)/shard_map/reduce_scatter | solution.py:180
  677.9 652.2 %reduce-scatter.7.cloned.1.call-done = f32[24,768]{1,0:T(8,128)} async-done(((f32[3072,768]{1,0:T(8,128)}), f32[24,768]{1,0:T(8,128)}) %reduce-scatter.7.cloned.1.call-update) | async-done | bytes 73744 | tf_op jit(solution)/shard_map/reduce_scatter | solution.py:251
  (275 shorter events, 113.7 us)
Async XLA Ops:
  7.2 318.0 %copy-start = (f32[768,16]{0,1:T(8,128)S(1)}, f32[768,16]{0,1:T(8,128)}, u32[]{:S(2)}) copy-start(f32[768,16]{0,1:T(8,128)} %param.17) | copy-start | bytes 147460
  7.2 204.9 %all-gather.3.cloned.1.call-start = ((), (), s32[]{:S(2)}) async-start(), calls=%async_computation.8 | async-start | bytes 4755456 | tf_op jit(solution)/shard_map/all_gather | solution.py:65
  7.9 270.5 %all-gather.5.cloned.1.call-start = ((), (), s32[]{:S(2)}) async-start(), calls=%async_computation.9 | async-start | bytes 3538944 | tf_op jit(solution)/shard_map/all_gather | solution.py:74
  9.6 204.7 %copy-start.63 = (f32[128]{0:T(128)}, f32[128]{0:T(128)S(1)}, u32[]{:S(2)}) copy-start(f32[128]{0:T(128)S(1)} %fusion.181) | copy-start | bytes 1540
  9.6 204.7 %copy-start.24 = (bf16[1,128,768]{2,1,0:T(8,128)(2,1)S(1)}, bf16[1,128,768]{2,1,0:T(8,128)(2,1)}, u32[]{:S(2)}) copy-start(bf16[1,128,768]{2,1,0:T(8,128)(2,1)} %param.11) | copy-start | bytes 589828
  9.6 204.7 %copy-start.51 = (f32[768]{0:T(1024)S(1)}, f32[768]{0:T(1024)}, u32[]{:S(2)}) copy-start(f32[768]{0:T(1024)} %param.13) | copy-start | bytes 9220
  246.1 54.0 %copy-start.60 = (s32[128]{0:T(128)}, s32[128]{0:T(128)S(1)}, u32[]{:S(2)}) copy-start(s32[128]{0:T(128)S(1)} %multiply_add_fusion) | copy-start | bytes 1540
  295.1 19.9 %slice-start = ((s8[4718592]{0:T(1024)(128)(4,1)}), s8[4194304]{0:T(1024)(128)(4,1)S(1)}, s32[]{:S(2)}) async-start(s8[4718592]{0:T(1024)(128)(4,1)} %bitcast.301), calls=%async_computation.14 | async-start | bytes 8388608
  300.1 70.8 %copy-start.12 = (f32[128,768]{1,0:T(8,128)}, f32[128,768]{1,0:T(8,128)S(1)}, u32[]{:S(2)}) copy-start(f32[128,768]{1,0:T(8,128)S(1)} %get-tuple-element.58) | copy-start | bytes 1179652
  300.1 70.8 %copy-start.55 = (f32[128]{0:T(128)}, f32[128]{0:T(128)S(1)}, u32[]{:S(2)}) copy-start(f32[128]{0:T(128)S(1)} %fusion.182) | copy-start | bytes 1540
  300.1 18.1 %slice-start.4 = ((s8[4718592]{0:T(1024)(128)(4,1)}), s8[4194304]{0:T(1024)(128)(4,1)S(1)}, s32[]{:S(2)}) async-start(s8[4718592]{0:T(1024)(128)(4,1)} %bitcast.347), calls=%async_computation.18 | async-start | bytes 8388608
  320.9 13.5 %all-to-all-start.1 = ((bf16[16,1,16,768]{3,2,1,0:T(8,128)(2,1)}), bf16[16,1,16,768]{3,2,1,0:T(8,128)(2,1)}, u32[]{:S(2)}, u32[]{:S(2)}) async-start(bf16[16,1,16,768]{3,2,1,0:T(8,128)(2,1)} %fusion.56), calls=%async_computation.1 | async-start | bytes 786432 | tf_op jit(solution)/shard_map/all_to_all | solution.py:149
  325.1 167.9 %reduce-scatter.5.cloned.1.call-start = ((), (), s32[]{:S(2)}) async-start(), calls=%async_computation.10 | async-start | bytes 3538944 | tf_op jit(solution)/shard_map/reduce_scatter | solution.py:234
  325.7 44.4 %copy-start.59 = (f32[128]{0:T(128)}, f32[128]{0:T(128)S(1)}, u32[]{:S(2)}) copy-start(f32[128]{0:T(128)S(1)} %fusion.166) | copy-start | bytes 1540
  334.4 22.0 %slice-start.2 = ((s8[4718592]{0:T(1024)(128)(4,1)}), s8[4194304]{0:T(1024)(128)(4,1)S(1)}, s32[]{:S(2)}) async-start(s8[4718592]{0:T(1024)(128)(4,1)} %bitcast.303), calls=%async_computation.16 | async-start | bytes 8388608
  335.9 34.2 %copy-start.58 = (f32[128]{0:T(128)}, f32[128]{0:T(128)S(1)}, u32[]{:S(2)}) copy-start(f32[128]{0:T(128)S(1)} %get-tuple-element.59) | copy-start | bytes 1540
  335.9 34.2 %copy-start.62 = (f32[128]{0:T(128)}, f32[128]{0:T(128)S(1)}, u32[]{:S(2)}) copy-start(f32[128]{0:T(128)S(1)} %get-tuple-element.13) | copy-start | bytes 1540
  415.7 175.7 %reduce-scatter.11.cloned.1.call-start = ((), (), s32[]{:S(2)}) async-start(), calls=%async_computation.13 | async-start | bytes 5308416 | tf_op jit(solution)/shard_map/reduce_scatter | solution.py:183
  423.0 252.7 %reduce-scatter.9.cloned.1.call-start = ((), (), s32[]{:S(2)}) async-start(), calls=%async_computation.12 | async-start | bytes 5308416 | tf_op jit(solution)/shard_map/reduce_scatter | solution.py:180
  428.1 902.0 %reduce-scatter.7.cloned.1.call-start = ((), (), s32[]{:S(2)}) async-start(), calls=%async_computation.11 | async-start | bytes 9510912 | tf_op jit(solution)/shard_map/reduce_scatter | solution.py:251
  433.1 60.0 %copy-start.64 = (f32[128]{0:T(128)S(1)}, f32[128]{0:T(128)}, u32[]{:S(2)}) copy-start(f32[128]{0:T(128)} %copy-done.63) | copy-start | bytes 1540
  520.0 70.5 %copy-start.67 = (f32[128]{0:T(128)S(1)}, f32[128]{0:T(128)}, u32[]{:S(2)}) copy-start(f32[128]{0:T(128)} %copy-done.66) | copy-start | bytes 1540
  520.0 70.5 %copy-start.14 = (f32[128,768]{1,0:T(8,128)S(1)}, f32[128,768]{1,0:T(8,128)}, u32[]{:S(2)}) copy-start(f32[128,768]{1,0:T(8,128)} %copy-done.13) | copy-start | bytes 1179652
  590.5 739.6 %copy-start.1 = (f32[768,16]{0,1:T(8,128)S(1)}, f32[768,16]{0,1:T(8,128)}, u32[]{:S(2)}) copy-start(f32[768,16]{0,1:T(8,128)} %param.17) | copy-start | bytes 147460
  (59 other events, 214.8 us)
Sparse Core Ops, SparseCore 0:
  9.7 202.2 all-gather.2
  217.0 61.4 all-gather.4
  415.8 77.1 reduce-scatter.4
  497.4 87.3 reduce-scatter.10
  588.6 87.0 reduce-scatter.8
  678.6 651.4 reduce-scatter.6
where the time goes:
time: 1340 us
  waiting for transfers between devices  1030 us (77%)
  blocking collectives  107 us (8%)
  matrix products  89.6 us (7%)
  local copies, waits for them, and re-layouts  52.2 us (4%)
  other arithmetic  38.9 us (3%)
  between operations  15.4 us (1%)
    reduce_scatter x1, waiting for transfers between devices, body(): lax.psum_scatter(weight_grad, ('ctx', 'exp'), scatter_dimension=0, tiled=...  652 us
    all_gather x1, waiting for transfers between devices, body(): lax.all_gather(attn_weight, ('ctx', 'exp'), axis=0, tiled=True)  202 us
    reduce_scatter x1, waiting for transfers between devices, body(): lax.psum_scatter(in_local.astype(jnp.bfloat16), 'ctx', scatter_dimension=...  82.1 us
    psum x1, blocking collectives, body(): lax.psum((attn_norm_local, moe_norm_local, router_local, jnp.concatenate(...  69.1 us
    reduce_scatter x1, waiting for transfers between devices, body(): lax.psum_scatter(kv_terms.astype(jnp.bfloat16), 'ctx', scatter_dimension=...  53.2 us
    all_gather x1, waiting for transfers between devices, body(): gathered = lax.all_gather(projected[1:], 'ctx', axis=1, tiled=True)  29.9 us
  transfers between devices with their start and end apart: 7, of which 6 were waited for; matrix products, arithmetic and copies ran while one was open for 7% of the time, Pallas kernels for 0%

commit v1 on v0

v1 whole, which is shorter than its diff:
```python
from functools import partial
import math

import jax
import jax.numpy as jnp
from jax import lax
from jax.experimental import pallas as pl
from jax.experimental.pallas import tpu as pltpu
from jax.sharding import PartitionSpec as P

f32 = jnp.float32
bf16 = jnp.bfloat16
eps_norm = 1e-06
highest = lax.Precision.HIGHEST
bucket_edges = [
    edge if edge <= 16 else int(math.ceil(16.0 * 8.0 ** ((edge - 16) / 16.0)))
    for edge in range(1, 32)
]
masked = -1e30
head_size = 64
own_heads = 3
width_own = own_heads * head_size
half_block = 64
block_count = 16
query_blocks = 8
lanes_step = 256
vmem_bytes = 56 * 1024 * 1024

offsets = [(dz, dx) for dz in range(2) for dx in range(4)]


def gather_perm(dz, dx):
    return [(4 * z + x, 4 * (z ^ dz) + (x + dx) % 4) for z in range(2) for x in range(4)]


def scatter_perm(dz, dx):
    return [(4 * z + x, 4 * (z ^ dz) + (x - dx) % 4) for z in range(2) for x in range(4)]


def dot_nt(left, right):
    return lax.dot_general(left, right, (((1,), (1,)), ((), ())), preferred_element_type=f32)


def dot_tn(left, right):
    return lax.dot_general(left, right, (((0,), (0,)), ((), ())), preferred_element_type=f32)


def dot_nn(left, right):
    return jnp.dot(left, right, preferred_element_type=f32)


def block_places(me_ref, order_ref):
    me = me_ref[0]
    z, x = me // 4, me % 4
    places = []
    for dz, dx in offsets:
        source = 4 * ((z + dz) % 2) + (x - dx + 4) % 4
        places += [order_ref[2 * source], order_ref[2 * source + 1]]
    return places


def tile_class(places, query_block, key_block):
    return jnp.clip(places[query_block] - places[key_block], -1, 3) + 1


def tile_distance(step):
    key_row = lax.broadcasted_iota(jnp.int32, (half_block, 128), 0)
    query_row = lax.broadcasted_iota(jnp.int32, (half_block, 128), 1) & (half_block - 1)
    return step * half_block + query_row - key_row


def attend_kernel(
    me_ref, order_ref, table_ref, normed_ref, wq_ref, wk_ref, wv_ref,
    out_ref, q_ref, k_ref, v_ref, log_ref, tiles_ref, scores_ref,
):
    places = block_places(me_ref, order_ref)
    first_head = (me_ref[0] % 4) * own_heads
    for head in range(own_heads):
        tiles_ref[head, 0] = jnp.full((half_block, 128), masked, f32)
        tiles_ref[head, 4] = jnp.full((half_block, 128), table_ref[31, first_head + head], f32)
    for step in range(3):
        distance = tile_distance(step)
        terms = [
            jnp.full((half_block, 128), table_ref[0, first_head + head], f32)
            for head in range(own_heads)
        ]
        for bucket, edge in enumerate(bucket_edges, 1):
            beyond = distance >= edge
            for head in range(own_heads):
                terms[head] = jnp.where(beyond, table_ref[bucket, first_head + head], terms[head])
        for head in range(own_heads):
            tiles_ref[head, step + 1] = (
                jnp.where(distance >= 0, terms[head], masked) if step == 0 else terms[head]
            )
    normed = normed_ref[...]
    k_ref[...] = dot_nn(normed, wk_ref[...]).astype(bf16)
    v_ref[...] = dot_nn(normed, wv_ref[...]).astype(bf16)
    q_ref[...] = dot_nn(normed[: query_blocks * half_block], wq_ref[...]).astype(bf16) * bf16(0.125)
    first_half = lax.broadcasted_iota(jnp.int32, (half_block, 128), 1) < half_block
    for head in range(own_heads):
        columns = slice(head * head_size, (head + 1) * head_size)
        keys, values = k_ref[:, columns], v_ref[:, columns]
        for part in range(query_blocks * half_block // lanes_step):
            lanes = slice(part * lanes_step, (part + 1) * lanes_step)
            add_bias(places, tiles_ref, scores_ref, first_half, head, part,
                     dot_nt(keys, q_ref[lanes, columns]))
            scores = scores_ref[...]
            peak = jnp.max(scores, axis=0, keepdims=True)
            raised = jnp.exp(scores - peak)
            total = jnp.sum(raised, axis=0, keepdims=True)
            probs = (raised * (1.0 / total)).astype(bf16)
            out_ref[columns, lanes] = dot_tn(values, probs).astype(bf16)
            log_ref[head, :, lanes] = peak + jnp.log(total)


def add_bias(places, tiles_ref, scores_ref, first_half, head, part, raw):
    for key_block in range(block_count):
        rows = slice(key_block * half_block, (key_block + 1) * half_block)
        for group in range(lanes_step // 128):
            lanes = slice(group * 128, (group + 1) * 128)
            query_block = part * (lanes_step // half_block) + 2 * group
            left = tile_class(places, query_block, key_block)
            right = tile_class(places, query_block + 1, key_block)
            scores_ref[rows, lanes] = raw[rows, lanes] + jnp.where(
                first_half, tiles_ref[head, left], tiles_ref[head, right]
            )


def attend_back_kernel(
    me_ref, order_ref, q_ref, k_ref, v_ref, grad_ref, log_ref, tiles_ref,
    dq_ref, dk_ref, dv_ref, table_ref, scores_ref, sums_ref,
):
    places = block_places(me_ref, order_ref)
    first_half = lax.broadcasted_iota(jnp.int32, (half_block, 128), 1) < half_block
    buckets = []
    for step in range(3):
        distance = tile_distance(step)
        counted = jnp.zeros((half_block, 128), jnp.int32)
        for edge in bucket_edges:
            counted = counted + (distance >= edge).astype(jnp.int32)
        buckets.append(counted)
    for head in range(own_heads):
        columns = slice(head * head_size, (head + 1) * head_size)
        keys, values = k_ref[:, columns], v_ref[:, columns]
        sums_ref[...] = jnp.zeros_like(sums_ref)
        key_sum = value_sum = None
        for part in range(query_blocks * half_block // lanes_step):
            lanes = slice(part * lanes_step, (part + 1) * lanes_step)
            queries, grads = q_ref[lanes, columns], grad_ref[lanes, columns]
            add_bias(places, tiles_ref, scores_ref, first_half, head, part, dot_nt(keys, queries))
            probs = jnp.exp(scores_ref[...] - log_ref[head, :, lanes])
            probs_grad = dot_nt(values, grads)
            row_dot = jnp.sum(probs * probs_grad, axis=0, keepdims=True)
            score_grad = probs * (probs_grad - row_dot)
            scores_ref[...] = score_grad
            low = score_grad.astype(bf16)
            value_part = dot_nn(probs.astype(bf16), grads)
            key_part = dot_nn(low, queries)
            value_sum = value_part if value_sum is None else value_sum + value_part
            key_sum = key_part if key_sum is None else key_sum + key_part
            dq_ref[columns, lanes] = (dot_tn(keys, low) * 0.125).astype(bf16)
            for key_block in range(block_count):
                rows = slice(key_block * half_block, (key_block + 1) * half_block)
                for group in range(lanes_step // 128):
                    query_block = part * (lanes_step // half_block) + 2 * group
                    left = tile_class(places, query_block, key_block)
                    right = tile_class(places, query_block + 1, key_block)
                    tile = scores_ref[rows, group * 128 : (group + 1) * 128]
                    sums_ref[left] += jnp.where(first_half, tile, 0.0)
                    sums_ref[right] += jnp.where(first_half, 0.0, tile)
        dk_ref[:, columns] = key_sum.astype(bf16)
        dv_ref[:, columns] = value_sum.astype(bf16)
        for bucket in range(32):
            found = [jnp.where(buckets[step] == bucket, sums_ref[step + 1], 0.0) for step in range(3)]
            if bucket == 31:
                found.append(sums_ref[4])
            table_ref[head, bucket : bucket + 1, :] = jnp.sum(sum(found), axis=0, keepdims=True)


def in_smem():
    return pl.BlockSpec(memory_space=pltpu.SMEM)


def in_vmem():
    return pl.BlockSpec(memory_space=pltpu.VMEM)


def attend(me, order, table, normed_all, wq, wk, wv):
    rows = normed_all.shape[0]
    shapes = [
        ((width_own, rows // 2), bf16),
        ((rows // 2, width_own), bf16),
        ((rows, width_own), bf16),
        ((rows, width_own), bf16),
        ((own_heads, 1, rows // 2), f32),
        ((own_heads, 5, half_block, 128), f32),
    ]
    return pl.pallas_call(
        attend_kernel,
        out_shape=[jax.ShapeDtypeStruct(shape, kind) for shape, kind in shapes],
        in_specs=[in_smem()] * 3 + [in_vmem()] * 4,
        out_specs=[in_vmem()] * len(shapes),
        scratch_shapes=[pltpu.VMEM((rows, lanes_step), f32)],
        compiler_params=pltpu.CompilerParams(vmem_limit_bytes=vmem_bytes),
        name="attend",
    )(me, order, table, normed_all, wq, wk, wv)


def attend_back(me, order, q, k, v, grads, logs, tiles):
    rows = k.shape[0]
    shapes = [
        ((width_own, rows // 2), bf16),
        ((rows, width_own), bf16),
        ((rows, width_own), bf16),
        ((own_heads, 32, 128), f32),
    ]
    return pl.pallas_call(
        attend_back_kernel,
        out_shape=[jax.ShapeDtypeStruct(shape, kind) for shape, kind in shapes],
        in_specs=[in_smem()] * 2 + [in_vmem()] * 6,
        out_specs=[in_vmem()] * len(shapes),
        scratch_shapes=[
            pltpu.VMEM((rows, lanes_step), f32),
            pltpu.VMEM((5, half_block, 128), f32),
        ],
        compiler_params=pltpu.CompilerParams(vmem_limit_bytes=vmem_bytes),
        name="attend_back",
    )(me, order, q, k, v, grads, logs, tiles)


def swap(chunks, axis):
    return lax.all_to_all(chunks, axis, split_axis=0, concat_axis=0, tiled=True)


def spread(part, axis, count):
    return swap(jnp.broadcast_to(part[None], (count,) + part.shape), axis)


def gelu(u):
    return jax.nn.gelu(u, approximate=True)


def body(
    hidden_in,
    out_grad,
    attn_norm,
    attn_weight,
    bias_table,
    moe_norm,
    router,
    expert_in,
    expert_out,
    expert_ids,
    block_order,
):
    width = attn_norm.shape[0]
    ctx_count, exp_count = 8, 16
    me = lax.axis_index("ctx")
    x_index = me % 4
    z_index = me // 4
    tokens = hidden_in.shape[1]
    expert_count = router.shape[1]
    capacity = 2 * tokens // expert_count
    me_array = me.astype(jnp.int32).reshape(1)
    order = block_order[0]

    inputs = hidden_in[0].astype(f32)
    scale_one = lax.rsqrt(jnp.mean(inputs * inputs, axis=-1, keepdims=True) + eps_norm)
    scaled_one = inputs * scale_one
    normed_low = (scaled_one * attn_norm).astype(bf16)
    normed_all = jnp.concatenate(
        [normed_low]
        + [lax.ppermute(normed_low, "ctx", gather_perm(dz, dx)) for dz, dx in offsets[1:]],
        axis=0,
    )
    shard_rows = attn_weight.shape[0]
    columns_ctx = spread(attn_weight, "ctx", ctx_count)
    qkv_own = lax.dynamic_slice_in_dim(columns_ctx[:6], x_index * width_own, width_own, 2)
    out_own = lax.dynamic_index_in_dim(columns_ctx, 6 + x_index // 2, 0, False)
    part_own = jnp.concatenate(
        [qkv_own.transpose(1, 0, 2).reshape(shard_rows, 6 * width_own), out_own], axis=1
    )
    parts_all = spread(part_own, "exp", exp_count)
    qkv_weights = (
        parts_all[:, :, : 6 * width_own]
        .reshape(exp_count, shard_rows, 3, 2, width_own)
        .transpose(2, 3, 0, 1, 4)
        .reshape(3, width, width_own)
    )
    out_weight = lax.dynamic_slice_in_dim(
        parts_all[:, :, 6 * width_own :], (x_index % 2) * 8, 8, 0
    ).reshape(width_own, width)

    attended, q, k, v, logs, tiles = attend(
        me_array, order, bias_table, normed_all, qkv_weights[0], qkv_weights[1], qkv_weights[2]
    )
    out_partial = dot_tn(attended, out_weight)
    out_blocks = out_partial.reshape(4, tokens, width)
    mid = inputs + out_blocks[0]
    out_low = out_blocks.astype(bf16)
    for dx in range(1, 4):
        mid = mid + lax.ppermute(out_low[dx], "ctx", scatter_perm(0, dx)).astype(f32)

    scale_two = lax.rsqrt(jnp.mean(mid * mid, axis=-1, keepdims=True) + eps_norm)
    scaled_two = mid * scale_two
    normed_two = scaled_two * moe_norm
    logits = jnp.dot(normed_two, router, precision=highest)
    router_prob = jax.nn.softmax(logits, axis=-1)
    chosen = expert_ids[0, :, 0]
    picked = chosen[:, None] == jnp.arange(expert_count, dtype=jnp.int32)[None, :]
    gate = jnp.sum(jnp.where(picked, router_prob, 0.0), axis=-1, keepdims=True)
    earlier = (
        jnp.arange(tokens, dtype=jnp.int32)[:, None] > jnp.arange(tokens, dtype=jnp.int32)[None, :]
    )
    same = chosen[:, None] == chosen[None, :]
    slot = jnp.sum((earlier & same).astype(jnp.int32), axis=1)
    targets = chosen * capacity + slot
    placing = (
        targets[:, None] == jnp.arange(expert_count * capacity, dtype=jnp.int32)[None, :]
    ).astype(bf16)
    cotangent = out_grad[0].astype(f32)
    sent = (gate * cotangent).astype(bf16)
    both = jnp.concatenate([normed_two.astype(bf16), sent], axis=1)
    outgoing = dot_tn(placing, both).astype(bf16).reshape(exp_count, capacity, 2 * width)
    arrived = swap(outgoing, "exp").reshape(exp_count * capacity, 2 * width)

    gathered = [arrived] + [
        lax.ppermute(arrived, "ctx", gather_perm(dz, dx)) for dz, dx in offsets[1:]
    ]

    w_in, w_out = expert_in[0], expert_out[0]
    rows_in, rows_grad = arrived[:, :width], arrived[:, width:]
    pre = dot_nn(rows_in, w_in)
    activated, gelu_pull = jax.vjp(gelu, pre)
    produced = dot_nn(activated.astype(bf16), w_out).astype(bf16)
    pre_grad = gelu_pull(dot_nt(rows_grad, w_out))[0].astype(bf16)
    row_grad = dot_nt(pre_grad, w_in).astype(bf16)
    returned = swap(
        jnp.concatenate([produced, row_grad], axis=1).reshape(exp_count, capacity, 2 * width), "exp"
    )
    home = dot_nn(placing, returned.reshape(exp_count * capacity, 2 * width))
    expert_result, rows_back = home[:, :width], home[:, width:]

    block_out = (mid + gate * expert_result).astype(bf16)[None]
    gate_grad = jnp.sum(cotangent * expert_result, axis=-1, keepdims=True)
    prob_grad = jnp.where(picked, gate_grad, 0.0)
    logit_grad = router_prob * (
        prob_grad - jnp.sum(router_prob * prob_grad, axis=-1, keepdims=True)
    )
    router_local = lax.dot_general(
        normed_two, logit_grad, (((0,), (0,)), ((), ())), precision=highest
    )
    normed_two_grad = rows_back + lax.dot_general(
        logit_grad, router, (((1,), (1,)), ((), ())), precision=highest
    )
    moe_norm_local = jnp.sum(normed_two_grad * scaled_two, axis=0)
    gained = normed_two_grad * moe_norm
    mid_grad = cotangent + scale_two * (
        gained - scaled_two * jnp.mean(gained * scaled_two, axis=-1, keepdims=True)
    )
    attn_grad = mid_grad.astype(bf16)
    attn_grad_half = jnp.concatenate(
        [attn_grad]
        + [lax.ppermute(attn_grad, "ctx", gather_perm(0, dx)) for dx in range(1, 4)],
        axis=0,
    )
    attended_grad = dot_nt(attn_grad_half, out_weight).astype(bf16)
    out_weight_grad = dot_nn(attended, attn_grad_half)
    dq, dk, dv, table_local = attend_back(
        me_array, order, q, k, v, attended_grad, logs, tiles
    )

    key_value_part = dot_nt(dk, qkv_weights[1]) + dot_nt(dv, qkv_weights[2])
    query_part = lax.dot_general(
        dq, qkv_weights[0], (((0,), (1,)), ((), ())), preferred_element_type=f32
    )
    half = query_part.shape[0]
    row_blocks = jnp.concatenate(
        [key_value_part[:half] + query_part, key_value_part[half:]], axis=0
    ).reshape(8, tokens, width)
    row_low = row_blocks.astype(bf16)
    normed_grad = row_blocks[0]
    for index, (dz, dx) in enumerate(offsets):
        if index:
            normed_grad = normed_grad + lax.ppermute(
                row_low[index], "ctx", scatter_perm(dz, dx)
            ).astype(f32)
    gained_one = normed_grad * attn_norm
    input_grad = (
        mid_grad
        + scale_one
        * (gained_one - scaled_one * jnp.mean(gained_one * scaled_one, axis=-1, keepdims=True))
    )[None]

    query_grad = lax.dot_general(
        normed_all[:half], dq, (((0,), (1,)), ((), ())), preferred_element_type=f32
    )
    qkv_grad = jnp.stack([query_grad, dot_tn(normed_all, dk), dot_tn(normed_all, dv)])
    attn_norm_local = jnp.sum(qkv_grad * qkv_weights.astype(f32), axis=(0, 2)) / attn_norm
    odd = x_index % 2
    out_low_grad = out_weight_grad.astype(bf16)
    half_width = width // 2
    kept = lax.dynamic_slice_in_dim(out_low_grad, odd * half_width, half_width, 1)
    given = lax.dynamic_slice_in_dim(out_low_grad, (1 - odd) * half_width, half_width, 1)
    pair = [(index, index ^ 1) for index in range(ctx_count)]
    taken = lax.ppermute(given, "ctx", pair)
    out_square = jnp.where(
        odd == 0,
        jnp.concatenate([kept, taken], axis=0),
        jnp.concatenate([taken, kept], axis=0),
    )
    weight_chunks = jnp.concatenate(
        [
            qkv_grad.astype(bf16)
            .reshape(6, exp_count, shard_rows, width_own)
            .transpose(1, 2, 0, 3)
            .reshape(exp_count, shard_rows, 6 * width_own),
            out_square.reshape(exp_count, shard_rows, half_width),
        ],
        axis=2,
    )
    table_grad = lax.dynamic_update_slice_in_dim(
        jnp.zeros(bias_table.shape, f32), jnp.sum(table_local, axis=-1).T, x_index * own_heads, 1
    )
    small = jnp.concatenate(
        [router_local.reshape(-1), table_grad.reshape(-1), attn_norm_local, moe_norm_local]
    )
    small_rows = 10
    chunk_width = 2 * width
    small = jnp.pad(small, (0, small_rows * chunk_width - small.shape[0])).reshape(
        small_rows, chunk_width
    )
    chunks = jnp.concatenate(
        [
            weight_chunks,
            jnp.broadcast_to(small.astype(bf16)[None], (exp_count, small_rows, chunk_width)),
        ],
        axis=1,
    )
    summed = jnp.sum(swap(chunks, "exp").astype(f32), axis=0)
    weight_sum, small_sum = summed[:shard_rows], summed[shard_rows:]
    qkv_sum = jnp.pad(
        weight_sum[:, : 6 * width_own].reshape(shard_rows, 6, width_own).transpose(1, 0, 2),
        ((0, 0), (0, 0), (0, half_width - width_own)),
    )
    out_sum = weight_sum[:, 6 * width_own :]
    to_out = jnp.where(
        jnp.arange(2, dtype=jnp.int32)[:, None, None] == x_index // 2, out_sum[None], 0.0
    )
    small_part = small_sum.reshape(-1, half_width)
    last = swap(
        jnp.concatenate(
            [
                jnp.concatenate([qkv_sum, to_out], axis=0),
                jnp.broadcast_to(small_part[None], (ctx_count,) + small_part.shape),
            ],
            axis=1,
        ),
        "ctx",
    )
    weight_last = last[:4, :shard_rows] + last[4:, :shard_rows]
    as_qkv = weight_last[:, :, :width_own].transpose(1, 0, 2).reshape(shard_rows, width)
    as_out = (weight_last[:2] + weight_last[2:]).transpose(1, 0, 2).reshape(shard_rows, width)
    attn_weight_grad = jnp.where(me < 6, as_qkv, as_out)
    small_last = jnp.sum(last[:, shard_rows:], axis=0).reshape(-1)
    router_size = router.size
    table_size = bias_table.size
    router_grad = small_last[:router_size].reshape(router.shape)
    small_rest = small_last[router_size:]
    bias_table_grad = small_rest[:table_size].reshape(bias_table.shape)
    attn_norm_grad = small_rest[table_size : table_size + width]
    moe_norm_grad = small_rest[table_size + width : table_size + 2 * width]

    hidden_own = w_in.shape[1] // ctx_count
    w_in_own = lax.dynamic_slice_in_dim(w_in, me * hidden_own, hidden_own, 1)
    w_out_own = lax.dynamic_slice_in_dim(w_out, me * hidden_own, hidden_own, 0)
    every = jnp.concatenate(gathered, axis=0)
    every_in, every_grad = every[:, :width], every[:, width:]
    pre_own = dot_nn(every_in, w_in_own)
    activated_own, own_pull = jax.vjp(gelu, pre_own)
    expert_out_grad = dot_tn(activated_own.astype(bf16), every_grad)[None]
    pre_grad_own = own_pull(dot_nt(every_grad, w_out_own))[0].astype(bf16)
    in_columns = dot_tn(every_in, pre_grad_own).reshape(ctx_count, width // ctx_count, hidden_own)
    in_low = in_columns.astype(bf16)
    expert_in_grad = lax.dynamic_update_slice_in_dim(
        jnp.zeros((width // ctx_count, ctx_count * hidden_own), f32),
        lax.dynamic_index_in_dim(in_columns, me, 0, False),
        me * hidden_own,
        1,
    )
    for step in range(1, ctx_count):
        given_rows = lax.dynamic_index_in_dim(in_low, (me + step) % ctx_count, 0, False)
        taken_rows = lax.ppermute(
            given_rows, "ctx", [(index, (index + step) % ctx_count) for index in range(ctx_count)]
        )
        source = (me - step + ctx_count) % ctx_count
        expert_in_grad = lax.dynamic_update_slice_in_dim(
            expert_in_grad, taken_rows.astype(f32), source * hidden_own, 1
        )
    return (
        block_out,
        input_grad,
        attn_norm_grad,
        attn_weight_grad,
        bias_table_grad,
        moe_norm_grad,
        router_grad,
        expert_in_grad[None],
        expert_out_grad,
    )


def solution(mesh):
    placed = (
        P("exp", "ctx", None),
        P("exp", "ctx", None),
        P(),
        P(("ctx", "exp"), None),
        P(),
        P(),
        P(),
        P("exp", None, None),
        P("exp", None, None),
        P("exp", "ctx", None),
        P("exp", None),
    )
    return jax.shard_map(
        body,
        mesh=mesh,
        in_specs=placed,
        out_specs=(
            P("exp", "ctx", None),
            P("exp", "ctx", None),
            P(),
            P(("ctx", "exp"), None),
            P(),
            P(),
            P(),
            P("exp", "ctx", None),
            P("exp", "ctx", None),
        ),
        check_vma=False,
    )
```

time: 1340 us -> 422 us (0.31)
  waiting for transfers between devices: 1030 us -> 138 us
  starting transfers between devices: 4.62 us -> 108 us
  blocking collectives: 107 us -> 18 us
  matrix products: 89.6 us -> 53.3 us
  Pallas kernels: 0 us -> 18.7 us
    reduce_scatter x4 -> x0, waiting for transfers between devices: 788 us -> none  [the longest x1 652 us: body(): lax.psum_scatter(weight_grad, ('ctx', 'exp'), scatter_dimension=0, tiled=...]
    all_gather x2 -> x0, waiting for transfers between devices: 232 us -> none  [the longest x1 202 us: body(): lax.all_gather(attn_weight, ('ctx', 'exp'), axis=0, tiled=True)]
    ppermute x0 -> x35, waiting for transfers between devices: none -> 98.7 us  [the longest x7 61.7 us: body(): lax.ppermute(arrived, 'ctx', gather_perm(dz, dx))]
    ppermute x0 -> x35, starting transfers between devices: none -> 79.6 us  [the longest x7 21.9 us: body(): lax.ppermute(given_rows, 'ctx', [(index, (index + step) % ctx_count) for...]
    psum x1 -> x0, blocking collectives: 69.1 us -> none  [body(): lax.psum((attn_norm_local, moe_norm_local, router_local, jnp.concatenate(...]
    dot_general x40 -> x19, matrix products: 89.1 us -> 52.8 us  [the longest x6 20.1 us: dot_tn(): lax.dot_general(left, right, (((0,), (0,)), ((), ())), preferred_element_...]
    all_to_all x1 -> x5, waiting for transfers between devices: 8.63 us -> 38.9 us  [swap(): return lax.all_to_all(chunks, axis, split_axis=0, concat_axis=0, tiled=True)]
    all_to_all x1 -> x5, starting transfers between devices: 4.21 us -> 28 us  [swap(): return lax.all_to_all(chunks, axis, split_axis=0, concat_axis=0, tiled=True)]
  transfers between devices with their start and end apart: 7 -> 40, of which waited for: 6 -> 16; matrix products, arithmetic and copies ran while one was open for 7% -> 15% of each run, Pallas kernels for 0% -> 0%
where the time goes in v1:
time: 422 us; the launch traced here: 417 us
  waiting for transfers between devices  138 us (33%)
  starting transfers between devices  108 us (26%)
  matrix products  53.3 us (13%)
  local copies, waits for them, and re-layouts  51 us (12%)
  other arithmetic  28.3 us (7%)
  Pallas kernels  18.7 us (4%)
  blocking collectives  18 us (4%)
    ppermute x7, waiting for transfers between devices, body(): lax.ppermute(arrived, 'ctx', gather_perm(dz, dx))  61.7 us
    all_to_all x5, waiting for transfers between devices, swap(): return lax.all_to_all(chunks, axis, split_axis=0, concat_axis=0, tiled=True)  38.9 us
    all_to_all x5, starting transfers between devices, swap(): return lax.all_to_all(chunks, axis, split_axis=0, concat_axis=0, tiled=True)  28 us
    ppermute x7, starting transfers between devices, body(): lax.ppermute(given_rows, 'ctx', [(index, (index + step) % ctx_count) for...  21.9 us
    ppermute x7, waiting for transfers between devices, body(): lax.ppermute(normed_low, 'ctx', gather_perm(dz, dx))  21.8 us
    unnamed x90, local copies, waits for them, and re-layouts  21.2 us
    dot_general x6, matrix products, dot_tn(): lax.dot_general(left, right, (((0,), (0,)), ((), ())), preferred_element_...  20.1 us
    all_to_all x1, blocking collectives, swap(): return lax.all_to_all(chunks, axis, split_axis=0, concat_axis=0, tiled=True)  18 us
  transfers between devices with their start and end apart: 40, of which 16 were waited for; matrix products, arithmetic and copies ran while one was open for 15% of the time, Pallas kernels for 0%

profile of v1, /device:TPU:0, one launch (start us, length us, event | category | flops | bytes accessed | tf_op | source)
XLA Modules:
  0.0 416.7 jit_solution(3094518505210989009)
XLA Ops:
  2.2 7.8 %all-to-all-start = ((bf16[8,24,768]{2,1,0:T(8,128)(2,1)}), bf16[8,24,768]{2,1,0:T(8,128)(2,1)S(1)}, u32[]{:S(2)}, u32[]{:S(2)}) async-start(bf16[8,24,768]{2,1,0:T(8,128)(2,1)} %broadcast_in_dim.123), calls=%async_computation | async-start | bytes 589824 | tf_op jit(solution)/shard_map/all_to_all | solution.py:232
  11.1 8.1 %all-to-all-done = bf16[8,24,768]{2,1,0:T(8,128)(2,1)S(1)} async-done(((bf16[8,24,768]{2,1,0:T(8,128)(2,1)}), bf16[8,24,768]{2,1,0:T(8,128)(2,1)S(1)}, u32[]{:S(2)}, u32[]{:S(2)}) %all-to-all-start) | async-done | bytes 294944 | tf_op jit(solution)/shard_map/all_to_all | solution.py:232
  20.7 5.0 %all-to-all-start.1 = ((bf16[16,24,1920]{2,1,0:T(8,128)(2,1)}), bf16[16,24,1920]{2,1,0:T(8,128)(2,1)S(1)}, u32[]{:S(2)}, u32[]{:S(2)}) async-start(bf16[16,24,1920]{2,1,0:T(8,128)(2,1)} %broadcast_in_dim.124), calls=%async_computation.1 | async-start | bytes 2949120 | tf_op jit(solution)/shard_map/all_to_all | solution.py:232
  35.0 5.1 %collective-permute-done = bf16[128,768]{1,0:T(8,128)(2,1)} collective-permute-done((bf16[128,768]{1,0:T(8,128)(2,1)}, bf16[128,768]{1,0:T(8,128)(2,1)}, u32[]{:S(2)}, u32[]{:S(2)}) %collective-permute-start) | collective-permute-done | bytes 196640 | tf_op jit(solution)/shard_map/ppermute | solution.py:273
  44.8 16.7 %collective-permute-done.3 = bf16[128,768]{1,0:T(8,128)(2,1)} collective-permute-done((bf16[128,768]{1,0:T(8,128)(2,1)}, bf16[128,768]{1,0:T(8,128)(2,1)}, u32[]{:S(2)}, u32[]{:S(2)}) %collective-permute-start.3) | collective-permute-done | bytes 196640 | tf_op jit(solution)/shard_map/ppermute | solution.py:273
  72.4 9.0 %attend.1 = (bf16[192,512]{1,0:T(8,128)(2,1)}, bf16[512,192]{1,0:T(8,128)(2,1)}, bf16[1024,192]{1,0:T(8,128)(2,1)}, bf16[1024,192]{1,0:T(8,128)(2,1)}, f32[3,1,512]{2,1,0:T(1,128)}, /*index=5*/f32[3,5,64,128]{3,2,1,0:T(8,128)}) custom-call(s32[1]{0:T(128)} %bitcast.1.me_ref, s32[16]{0:T(128)} %bitcast.179, f32[32,12]{1,0:T(8,128)} %copy.137.table_ref, ...), custom_call_target="tpu_custom_call" | custom-call | tf_op jit(solution)/shard_map/attend/pallas_call | solution.py:198
  87.2 7.6 %collective-permute-done.9 = bf16[128,768]{1,0:T(8,128)(2,1)S(1)} collective-permute-done((bf16[128,768]{1,0:T(8,128)(2,1)S(1)}, bf16[128,768]{1,0:T(8,128)(2,1)S(1)}, u32[]{:S(2)}, u32[]{:S(2)}) %collective-permute-start.9) | collective-permute-done | bytes 196640 | tf_op jit(solution)/shard_map/ppermute | solution.py:302
  96.8 18.0 %all_to_all.30 = bf16[16,16,1536]{2,1,0:T(8,128)(2,1)S(1)} all-to-all(bf16[16,16,1536]{2,1,0:T(8,128)(2,1)S(1)} %bitcast.162), channel_id=1, replica_groups=mesh['ctx'=8,'exp'=16] {'exp'}, dimensions={0} | all-to-all | bytes 1572864 | tf_op jit(solution)/shard_map/all_to_all | solution.py:232
  117.9 8.4 %fusion.48 = bf16[256,768]{1,0:T(8,128)(2,1)S(1)} fusion(bf16[1,768,3072]{2,1,0:T(8,128)(2,1)} %param.18, f32[256,3072]{1,0:T(8,128)} %fusion.6, bf16[1,3072,768]{2,1,0:T(8,128)(2,1)} %param.19, bf16[256,1536]{1,0:T(8,128)(2,1)S(1)} %bitcast.151), kind=kOutput, calls=%fused_computation.52 | convolution fusion | flops 2431844352 | bytes 13369344 | tf_op jit(solution)/shard_map/dot_general | solution.py:41
  126.3 5.2 %fusion.51 = bf16[256,768]{1,0:T(8,128)(2,1)S(1)} fusion(bf16[1,3072,768]{2,1,0:T(8,128)(2,1)} %param.19, f32[256,3072]{1,0:T(8,128)} %fusion.6), kind=kOutput, calls=%fused_computation.53 | convolution fusion | flops 1215234048 | bytes 8257536 | tf_op jit(solution)/shard_map/dot_general | solution.py:49
  164.5 11.8 %collective-permute-done.22 = bf16[256,1536]{1,0:T(8,128)(2,1)} collective-permute-done((bf16[256,1536]{1,0:T(8,128)(2,1)S(1)}, bf16[256,1536]{1,0:T(8,128)(2,1)}, u32[]{:S(2)}, u32[]{:S(2)}) %collective-permute-start.22) | collective-permute-done | bytes 786464 | tf_op jit(solution)/shard_map/ppermute | solution.py:328
  189.6 28.6 %collective-permute-done.25 = bf16[256,1536]{1,0:T(8,128)(2,1)} collective-permute-done((bf16[256,1536]{1,0:T(8,128)(2,1)S(1)}, bf16[256,1536]{1,0:T(8,128)(2,1)}, u32[]{:S(2)}, u32[]{:S(2)}) %collective-permute-start.25) | collective-permute-done | bytes 786464 | tf_op jit(solution)/shard_map/ppermute | solution.py:328
  218.2 6.9 %collective-permute-start.10 = (bf16[128,768]{1,0:T(8,128)(2,1)}, bf16[128,768]{1,0:T(8,128)(2,1)}, u32[]{:S(2)}, u32[]{:S(2)}) collective-permute-start(bf16[128,768]{1,0:T(8,128)(2,1)} %fusion.165), channel_id=1, source_target_pairs={{0,16},{16,32},{32,48},{48,0},{64,80},{80,96},{96,112},{112,64},{1... | collective-permute-start | bytes 589832 | tf_op jit(solution)/shard_map/ppermute | solution.py:364
  227.2 16.7 %collective-permute-done.26 = bf16[256,1536]{1,0:T(8,128)(2,1)S(1)} collective-permute-done((bf16[256,1536]{1,0:T(8,128)(2,1)S(1)}, bf16[256,1536]{1,0:T(8,128)(2,1)S(1)}, u32[]{:S(2)}, u32[]{:S(2)}) %collective-permute-start.26) | collective-permute-done | bytes 786464 | tf_op jit(solution)/shard_map/ppermute | solution.py:328
  245.8 5.5 %fusion.28 = f32[2048,384]{1,0:T(8,128)} fusion(bf16[2048,1536]{1,0:T(8,128)(2,1)} %constant_dynamic-update-slice_fusion.8, bf16[1,768,3072]{2,1,0:T(8,128)(2,1)} %param.18, s32[]{:T(128)S(6)} %select_n.180), kind=kOutput, calls=%fused_computation.35 | convolution fusion | flops 1207959552 | bytes 6881284 | tf_op jit(solution)/shard_map/dot_general | solution.py:49
  251.3 8.0 %fusion.26 = f32[768,384]{1,0:T(8,128)S(1)} fusion(bf16[2048,1536]{1,0:T(8,128)(2,1)} %constant_dynamic-update-slice_fusion.8, f32[2048,384]{1,0:T(8,128)} %fusion.28, bf16[1,3072,768]{2,1,0:T(8,128)(2,1)} %param.19, s32[]{:T(128)S(6)} %select_n.180), kind=kOutput, calls=%fused_computation.33 | convolution fusion | flops 2431647744 | bytes 11206660 | tf_op jit(solution)/shard_map/dot_general | solution.py:45
  259.4 5.4 %fusion.45 = f32[1,384,768]{2,1,0:T(8,128)} fusion(bf16[2048,1536]{1,0:T(8,128)(2,1)} %constant_dynamic-update-slice_fusion.8, f32[2048,384]{1,0:T(8,128)} %fusion.28), kind=kOutput, calls=%fused_computation.51 | convolution fusion | flops 1215037440 | bytes 7471104 | tf_op jit(solution)/shard_map/dot_general | solution.py:45
  265.0 7.1 %collective-permute-start.29 = (bf16[96,384]{1,0:T(8,128)(2,1)S(1)}, bf16[96,384]{1,0:T(8,128)(2,1)S(1)}, u32[]{:S(2)}, u32[]{:S(2)}) collective-permute-start(bf16[96,384]{1,0:T(8,128)(2,1)S(1)} %get-tuple-element.111), channel_id=1, source_target_pairs={{0,32},{16,48},{32,64},{48,80},{64,96},{80,112},{96,0},{112,16},{1... | collective-permute-start | bytes 221192 | tf_op jit(solution)/shard_map/ppermute | solution.py:493
  298.1 9.7 %attend_back.1 = (bf16[192,512]{1,0:T(8,128)(2,1)}, bf16[1024,192]{1,0:T(8,128)(2,1)}, bf16[1024,192]{1,0:T(8,128)(2,1)}, f32[3,32,128]{2,1,0:T(8,128)}) custom-call(s32[1]{0:T(128)} %bitcast.1.me_ref, s32[16]{0:T(128)} %bitcast.180, bf16[512,192]{1,0:T(8,128)(2,1)} %get-tuple-element.20.q_ref, bf16[1024,192]{1,0:T(8,128)(2,1)} %get-tuple-element.21.k_ref, ...), custom_call_target="tpu_custom_call" | custom-call | tf_op jit(solution)/shard_map/attend_back/pallas_call | solution.py:217
  341.7 5.1 %all-to-all-start.4 = ((bf16[16,34,1536]{2,1,0:T(8,128)(2,1)}), bf16[16,34,1536]{2,1,0:T(8,128)(2,1)}, u32[]{:S(2)}, u32[]{:S(2)}) async-start(bf16[16,34,1536]{2,1,0:T(8,128)(2,1)} %pad_maximum_fusion), calls=%async_computation.4 | async-start | bytes 3932160 | tf_op jit(solution)/shard_map/all_to_all | solution.py:232
  350.9 5.7 %collective-permute-start.18 = (bf16[128,768]{1,0:T(8,128)(2,1)S(1)}, bf16[128,768]{1,0:T(8,128)(2,1)S(1)}, u32[]{:S(2)}, u32[]{:S(2)}) collective-permute-start(bf16[128,768]{1,0:T(8,128)(2,1)S(1)} %get-tuple-element.93), channel_id=1, source_target_pairs={{0,96},{16,112},{32,64},{48,80},{64,32},{80,48},{96,0},{112,16},{1... | collective-permute-start | bytes 589832 | tf_op jit(solution)/shard_map/ppermute | solution.py:385
  364.0 19.2 %all-to-all-done.4 = bf16[16,34,1536]{2,1,0:T(8,128)(2,1)} async-done(((bf16[16,34,1536]{2,1,0:T(8,128)(2,1)}), bf16[16,34,1536]{2,1,0:T(8,128)(2,1)}, u32[]{:S(2)}, u32[]{:S(2)}) %all-to-all-start.4) | async-done | bytes 1671200 | tf_op jit(solution)/shard_map/all_to_all | solution.py:232
  391.2 6.4 %all-to-all-start.5 = ((f32[8,64,384]{2,1,0:T(8,128)}), f32[8,64,384]{2,1,0:T(8,128)S(1)}, u32[]{:S(2)}, u32[]{:S(2)}) async-start(f32[8,64,384]{2,1,0:T(8,128)} %pad_maximum_fusion.4), calls=%async_computation.5 | async-start | bytes 1572864 | tf_op jit(solution)/shard_map/all_to_all | solution.py:232
  403.8 8.8 %all-to-all-done.5 = f32[8,64,384]{2,1,0:T(8,128)S(1)} async-done(((f32[8,64,384]{2,1,0:T(8,128)}), f32[8,64,384]{2,1,0:T(8,128)S(1)}, u32[]{:S(2)}, u32[]{:S(2)}) %all-to-all-start.5) | async-done | bytes 786464 | tf_op jit(solution)/shard_map/all_to_all | solution.py:232
  (279 shorter events, 178.5 us)
Async XLA Ops:
  2.2 17.0 %all-to-all-start = ((bf16[8,24,768]{2,1,0:T(8,128)(2,1)}), bf16[8,24,768]{2,1,0:T(8,128)(2,1)S(1)}, u32[]{:S(2)}, u32[]{:S(2)}) async-start(bf16[8,24,768]{2,1,0:T(8,128)(2,1)} %broadcast_in_dim.123), calls=%async_computation | async-start | bytes 589824 | tf_op jit(solution)/shard_map/all_to_all | solution.py:232
  20.7 42.8 %all-to-all-start.1 = ((bf16[16,24,1920]{2,1,0:T(8,128)(2,1)}), bf16[16,24,1920]{2,1,0:T(8,128)(2,1)S(1)}, u32[]{:S(2)}, u32[]{:S(2)}) async-start(bf16[16,24,1920]{2,1,0:T(8,128)(2,1)} %broadcast_in_dim.124), calls=%async_computation.1 | async-start | bytes 2949120 | tf_op jit(solution)/shard_map/all_to_all | solution.py:232
  30.1 31.4 %collective-permute-start.3 = (bf16[128,768]{1,0:T(8,128)(2,1)}, bf16[128,768]{1,0:T(8,128)(2,1)}, u32[]{:S(2)}, u32[]{:S(2)}) collective-permute-start(bf16[128,768]{1,0:T(8,128)(2,1)} %get-tuple-element.90), channel_id=1, source_target_pairs={{0,64},{16,80},{32,96},{48,112},{64,0},{80,16},{96,32},{112,48},{1... | collective-permute-start | bytes 589832 | tf_op jit(solution)/shard_map/ppermute | solution.py:273
  31.3 31.2 %collective-permute-start.4 = (bf16[128,768]{1,0:T(8,128)(2,1)}, bf16[128,768]{1,0:T(8,128)(2,1)}, u32[]{:S(2)}, u32[]{:S(2)}) collective-permute-start(bf16[128,768]{1,0:T(8,128)(2,1)} %get-tuple-element.90), channel_id=1, source_target_pairs={{0,80},{16,96},{32,112},{48,64},{64,16},{80,32},{96,48},{112,0},{1... | collective-permute-start | bytes 589832 | tf_op jit(solution)/shard_map/ppermute | solution.py:273
  40.0 23.4 %collective-permute-start.5 = (bf16[128,768]{1,0:T(8,128)(2,1)}, bf16[128,768]{1,0:T(8,128)(2,1)S(1)}, u32[]{:S(2)}, u32[]{:S(2)}) collective-permute-start(bf16[128,768]{1,0:T(8,128)(2,1)} %get-tuple-element.90), channel_id=1, source_target_pairs={{0,96},{16,112},{32,64},{48,80},{64,32},{80,48},{96,0},{112,16},{1... | collective-permute-start | bytes 589832 | tf_op jit(solution)/shard_map/ppermute | solution.py:273
  41.0 22.5 %collective-permute-start.6 = (bf16[128,768]{1,0:T(8,128)(2,1)}, bf16[128,768]{1,0:T(8,128)(2,1)S(1)}, u32[]{:S(2)}, u32[]{:S(2)}) collective-permute-start(bf16[128,768]{1,0:T(8,128)(2,1)} %get-tuple-element.90), channel_id=1, source_target_pairs={{0,112},{16,64},{32,80},{48,96},{64,48},{80,0},{96,16},{112,32},{1... | collective-permute-start | bytes 589832 | tf_op jit(solution)/shard_map/ppermute | solution.py:273
  132.5 17.3 %all-to-all-start.3 = ((bf16[16,16,1536]{2,1,0:T(8,128)(2,1)}), bf16[16,16,1536]{2,1,0:T(8,128)(2,1)S(1)}, u32[]{:S(2)}, u32[]{:S(2)}) async-start(bf16[16,16,1536]{2,1,0:T(8,128)(2,1)} %bitcast.161), calls=%async_computation.3 | async-start | bytes 1572864 | tf_op jit(solution)/shard_map/all_to_all | solution.py:232
  136.9 22.5 %collective-permute-start.21 = (bf16[256,1536]{1,0:T(8,128)(2,1)S(1)}, bf16[256,1536]{1,0:T(8,128)(2,1)}, u32[]{:S(2)}, u32[]{:S(2)}) collective-permute-start(bf16[256,1536]{1,0:T(8,128)(2,1)S(1)} %bitcast.152), channel_id=1, source_target_pairs={{0,16},{16,32},{32,48},{48,0},{64,80},{80,96},{96,112},{112,64},{1... | collective-permute-start | bytes 2359304 | tf_op jit(solution)/shard_map/ppermute | solution.py:328
  137.4 38.8 %collective-permute-start.22 = (bf16[256,1536]{1,0:T(8,128)(2,1)S(1)}, bf16[256,1536]{1,0:T(8,128)(2,1)}, u32[]{:S(2)}, u32[]{:S(2)}) collective-permute-start(bf16[256,1536]{1,0:T(8,128)(2,1)S(1)} %bitcast.153), channel_id=1, source_target_pairs={{0,32},{16,48},{32,0},{48,16},{64,96},{80,112},{96,64},{112,80},{1... | collective-permute-start | bytes 2359304 | tf_op jit(solution)/shard_map/ppermute | solution.py:328
  140.9 37.4 %collective-permute-start.23 = (bf16[256,1536]{1,0:T(8,128)(2,1)S(1)}, bf16[256,1536]{1,0:T(8,128)(2,1)}, u32[]{:S(2)}, u32[]{:S(2)}) collective-permute-start(bf16[256,1536]{1,0:T(8,128)(2,1)S(1)} %bitcast.154), channel_id=1, source_target_pairs={{0,48},{16,0},{32,16},{48,32},{64,112},{80,64},{96,80},{112,96},{1... | collective-permute-start | bytes 2359304 | tf_op jit(solution)/shard_map/ppermute | solution.py:328
  140.9 43.1 %collective-permute-start.24 = (bf16[256,1536]{1,0:T(8,128)(2,1)S(1)}, bf16[256,1536]{1,0:T(8,128)(2,1)}, u32[]{:S(2)}, u32[]{:S(2)}) collective-permute-start(bf16[256,1536]{1,0:T(8,128)(2,1)S(1)} %bitcast.155), channel_id=1, source_target_pairs={{0,64},{16,80},{32,96},{48,112},{64,0},{80,16},{96,32},{112,48},{1... | collective-permute-start | bytes 2359304 | tf_op jit(solution)/shard_map/ppermute | solution.py:328
  144.5 73.7 %collective-permute-start.25 = (bf16[256,1536]{1,0:T(8,128)(2,1)S(1)}, bf16[256,1536]{1,0:T(8,128)(2,1)}, u32[]{:S(2)}, u32[]{:S(2)}) collective-permute-start(bf16[256,1536]{1,0:T(8,128)(2,1)S(1)} %bitcast.156), channel_id=1, source_target_pairs={{0,80},{16,96},{32,112},{48,64},{64,16},{80,32},{96,48},{112,0},{1... | collective-permute-start | bytes 2359304 | tf_op jit(solution)/shard_map/ppermute | solution.py:328
  159.4 84.6 %collective-permute-start.26 = (bf16[256,1536]{1,0:T(8,128)(2,1)S(1)}, bf16[256,1536]{1,0:T(8,128)(2,1)S(1)}, u32[]{:S(2)}, u32[]{:S(2)}) collective-permute-start(bf16[256,1536]{1,0:T(8,128)(2,1)S(1)} %bitcast.158), channel_id=1, source_target_pairs={{0,96},{16,112},{32,64},{48,80},{64,32},{80,48},{96,0},{112,16},{1... | collective-permute-start | bytes 2359304 | tf_op jit(solution)/shard_map/ppermute | solution.py:328
  176.3 68.6 %collective-permute-start.27 = (bf16[256,1536]{1,0:T(8,128)(2,1)S(1)}, bf16[256,1536]{1,0:T(8,128)(2,1)S(1)}, u32[]{:S(2)}, u32[]{:S(2)}) collective-permute-start(bf16[256,1536]{1,0:T(8,128)(2,1)S(1)} %bitcast.159), channel_id=1, source_target_pairs={{0,112},{16,64},{32,80},{48,96},{64,48},{80,0},{96,16},{112,32},{1... | collective-permute-start | bytes 2359304 | tf_op jit(solution)/shard_map/ppermute | solution.py:328
  178.4 115.7 %collective-permute-start.12 = (bf16[128,768]{1,0:T(8,128)(2,1)}, bf16[128,768]{1,0:T(8,128)(2,1)}, u32[]{:S(2)}, u32[]{:S(2)}) collective-permute-start(bf16[128,768]{1,0:T(8,128)(2,1)} %fusion.165), channel_id=1, source_target_pairs={{0,48},{16,0},{32,16},{48,32},{64,112},{80,64},{96,80},{112,96},{1... | collective-permute-start | bytes 589832 | tf_op jit(solution)/shard_map/ppermute | solution.py:364
  184.1 110.0 %collective-permute-start.11 = (bf16[128,768]{1,0:T(8,128)(2,1)}, bf16[128,768]{1,0:T(8,128)(2,1)}, u32[]{:S(2)}, u32[]{:S(2)}) collective-permute-start(bf16[128,768]{1,0:T(8,128)(2,1)} %fusion.165), channel_id=1, source_target_pairs={{0,32},{16,48},{32,0},{48,16},{64,96},{80,112},{96,64},{112,80},{1... | collective-permute-start | bytes 589832 | tf_op jit(solution)/shard_map/ppermute | solution.py:364
  218.2 75.9 %collective-permute-start.10 = (bf16[128,768]{1,0:T(8,128)(2,1)}, bf16[128,768]{1,0:T(8,128)(2,1)}, u32[]{:S(2)}, u32[]{:S(2)}) collective-permute-start(bf16[128,768]{1,0:T(8,128)(2,1)} %fusion.165), channel_id=1, source_target_pairs={{0,16},{16,32},{32,48},{48,0},{64,80},{80,96},{96,112},{112,64},{1... | collective-permute-start | bytes 589832 | tf_op jit(solution)/shard_map/ppermute | solution.py:364
  341.7 41.5 %all-to-all-start.4 = ((bf16[16,34,1536]{2,1,0:T(8,128)(2,1)}), bf16[16,34,1536]{2,1,0:T(8,128)(2,1)}, u32[]{:S(2)}, u32[]{:S(2)}) async-start(bf16[16,34,1536]{2,1,0:T(8,128)(2,1)} %pad_maximum_fusion), calls=%async_computation.4 | async-start | bytes 3932160 | tf_op jit(solution)/shard_map/all_to_all | solution.py:232
  348.2 37.2 %collective-permute-start.19 = (bf16[128,768]{1,0:T(8,128)(2,1)S(1)}, bf16[128,768]{1,0:T(8,128)(2,1)S(1)}, u32[]{:S(2)}, u32[]{:S(2)}) collective-permute-start(bf16[128,768]{1,0:T(8,128)(2,1)S(1)} %get-tuple-element.92), channel_id=1, source_target_pairs={{0,80},{16,96},{32,112},{48,64},{64,16},{80,32},{96,48},{112,0},{1... | collective-permute-start | bytes 589832 | tf_op jit(solution)/shard_map/ppermute | solution.py:385
  350.9 38.5 %collective-permute-start.18 = (bf16[128,768]{1,0:T(8,128)(2,1)S(1)}, bf16[128,768]{1,0:T(8,128)(2,1)S(1)}, u32[]{:S(2)}, u32[]{:S(2)}) collective-permute-start(bf16[128,768]{1,0:T(8,128)(2,1)S(1)} %get-tuple-element.93), channel_id=1, source_target_pairs={{0,96},{16,112},{32,64},{48,80},{64,32},{80,48},{96,0},{112,16},{1... | collective-permute-start | bytes 589832 | tf_op jit(solution)/shard_map/ppermute | solution.py:385
  356.6 41.1 %collective-permute-start.17 = (bf16[128,768]{1,0:T(8,128)(2,1)S(1)}, bf16[128,768]{1,0:T(8,128)(2,1)S(1)}, u32[]{:S(2)}, u32[]{:S(2)}) collective-permute-start(bf16[128,768]{1,0:T(8,128)(2,1)S(1)} %get-tuple-element.94), channel_id=1, source_target_pairs={{0,112},{16,64},{32,80},{48,96},{64,48},{80,0},{96,16},{112,32},{1... | collective-permute-start | bytes 589832 | tf_op jit(solution)/shard_map/ppermute | solution.py:385
  359.5 38.1 %collective-permute-start.16 = (bf16[128,768]{1,0:T(8,128)(2,1)S(1)}, bf16[128,768]{1,0:T(8,128)(2,1)S(1)}, u32[]{:S(2)}, u32[]{:S(2)}) collective-permute-start(bf16[128,768]{1,0:T(8,128)(2,1)S(1)} %get-tuple-element.91), channel_id=1, source_target_pairs={{0,64},{16,80},{32,96},{48,112},{64,0},{80,16},{96,32},{112,48},{1... | collective-permute-start | bytes 589832 | tf_op jit(solution)/shard_map/ppermute | solution.py:385
  362.6 35.1 %collective-permute-start.15 = (bf16[128,768]{1,0:T(8,128)(2,1)}, bf16[128,768]{1,0:T(8,128)(2,1)}, u32[]{:S(2)}, u32[]{:S(2)}) collective-permute-start(bf16[128,768]{1,0:T(8,128)(2,1)} %get-tuple-element.99), channel_id=1, source_target_pairs={{0,16},{16,32},{32,48},{48,0},{64,80},{80,96},{96,112},{112,64},{1... | collective-permute-start | bytes 589832 | tf_op jit(solution)/shard_map/ppermute | solution.py:385
  391.2 21.4 %all-to-all-start.5 = ((f32[8,64,384]{2,1,0:T(8,128)}), f32[8,64,384]{2,1,0:T(8,128)S(1)}, u32[]{:S(2)}, u32[]{:S(2)}) async-start(f32[8,64,384]{2,1,0:T(8,128)} %pad_maximum_fusion.4), calls=%async_computation.5 | async-start | bytes 1572864 | tf_op jit(solution)/shard_map/all_to_all | solution.py:232
  (54 other events, 741.9 us)
